TPU v7x, 256 devices: a whole 4x4x8 slice. The times are simulated.
256 devices in a mesh: view: 8 (over x, core), samp: 32 (over z, y).
Axes of the slice: x: 4, y: 4, z: 8, core: 2. Of those that a mesh axis runs over, the one named last changes fastest.
Arguments:
- view_data: bfloat16 [16, 16384, 2048], P('view', 'samp'), may hold values from -10 to 10
- init_coeffs: float32 [16, 2048, 128], P('view'), may hold values from -0.125 to 0.125
Outputs:
- shared_scores: float32 [16384, 128], P('samp')
- final_coeffs: float32 [16, 2048, 128], P('view', 'samp')
All inputs are finite; a program needn't handle non-finite values.
Results may differ from a plain program's by a relative error of at most 0.005.
Values may be sent and summed in bfloat16 or wider, within the bound.
A program may use at most 128 MiB of HBM per device.

v0:
```python
import jax
import jax.numpy as jnp
from jax import lax
from jax.sharding import PartitionSpec as P

OUTER = 2
INNER = 2
NS_ITERS = 12


HIGH = lax.Precision.HIGHEST
ridge_weight = 0.1
step_size = 0.5


def copy_for_each(x, axis):
    peers = lax.axis_size(axis)
    return lax.all_to_all(jnp.broadcast_to(x[None], (peers, *x.shape)), axis, 0, 0, tiled=True)


def of_everyone(x, axis):
    return copy_for_each(x, axis).sum(axis=0)


def split_up(x, dim, peers):
    lengths = x.shape
    parts = x.reshape(*lengths[:dim], peers, lengths[dim] // peers, *lengths[dim + 1 :])
    return jnp.moveaxis(parts, dim, 0)


def sent_and_summed(x, axis, dim):
    peers = lax.axis_size(axis)
    parts = lax.all_to_all(split_up(x, dim, peers), axis, 0, 0, tiled=True)
    return jnp.sum(parts, axis=0)


def laid_out(parts, dim):
    parts = jnp.moveaxis(parts, 0, dim)
    lengths = parts.shape
    return parts.reshape(*lengths[:dim], lengths[dim] * lengths[dim + 1], *lengths[dim + 2 :])


def gathered_copies(x, axis, dim):
    parts = copy_for_each(x, axis)
    return laid_out(parts, dim)


def newton_inverse(gram):
    size_k = gram.shape[0]
    eye_mat = jnp.eye(size_k, dtype=jnp.float32)
    shrunk = gram + jnp.trace(gram) / size_k * eye_mat
    scale = jnp.sqrt(jnp.sum(shrunk * shrunk))
    approx = shrunk / scale
    inverse = eye_mat
    for turn in range(NS_ITERS):
        factor = 0.5 * (3.0 * eye_mat - jnp.dot(inverse, approx, precision=HIGH))
        approx = jnp.dot(approx, factor, precision=HIGH)
        inverse = jnp.dot(factor, inverse, precision=HIGH)
    return (inverse, scale)


def make_scores(view_data, coeffs_low, total):
    local_sum = jnp.zeros((view_data.shape[1], coeffs_low.shape[2]), jnp.float32)
    for member in range(view_data.shape[0]):
        local_sum = local_sum + jnp.dot(
            view_data[member], coeffs_low[member], preferred_element_type=jnp.float32
        )
    summed = of_everyone(local_sum, "view")
    gram = of_everyone(jnp.dot(summed.T, summed, precision=HIGH), "samp")
    inverse, scale = newton_inverse(gram)
    return jnp.dot(summed, inverse, precision=HIGH) * jnp.sqrt(total / scale)


def grad_term(samples, weights_low, scores):
    resid = (jnp.dot(samples, weights_low, preferred_element_type=jnp.float32) - scores).astype(
        jnp.bfloat16
    )
    return lax.dot_general(
        samples, resid, (((0,), (0,)), ((), ())), preferred_element_type=jnp.float32
    )


def body(view_data, init_coeffs):
    total = view_data.shape[1] * lax.axis_size("samp")
    row_count = init_coeffs.shape[1] // lax.axis_size("samp")
    row_start = lax.axis_index("samp") * row_count
    own_coeffs = lax.dynamic_slice_in_dim(init_coeffs, row_start, row_count, 1)
    coeffs_low = init_coeffs.astype(jnp.bfloat16)
    scores = make_scores(view_data, coeffs_low, total)
    for outer_step in range(OUTER):
        for inner_step in range(INNER):
            terms = jnp.stack(
                [
                    grad_term(view_data[member], coeffs_low[member], scores)
                    for member in range(view_data.shape[0])
                ]
            )
            summed_grad = sent_and_summed(terms, "samp", 1)
            own_coeffs = own_coeffs - step_size * (summed_grad / total + ridge_weight * own_coeffs)
            coeffs_low = gathered_copies(own_coeffs.astype(jnp.bfloat16), "samp", 1)
        scores = make_scores(view_data, coeffs_low, total)
    return (scores, own_coeffs)


def solution(mesh):
    in_specs = (P("view", "samp", None), P("view", None, None))
    out_specs = (P("samp", None), P("view", "samp", None))
    return jax.shard_map(body, mesh=mesh, in_specs=in_specs, out_specs=out_specs, check_vma=False)
```

profile of v0, /device:TPU:1, one launch (start us, length us, event | category | flops | bytes accessed | tf_op | source)
XLA Modules:
  0.0 686.0 jit_solution(10328658307843747942)
XLA Ops:
  0.6 1.9 convert_element_type.42
  2.5 2.3 fusion.12
  5.7 32.1 %all_to_all.70 = f32[8,512,128]{2,1,0:T(8,128)S(1)} all-to-all(f32[8,512,128]{2,1,0:T(8,128)S(1)} %broadcast_in_dim.24), channel_id=1, replica_groups=mesh['view'=8,'samp'=32] {'view'}, dimensions={0} | all-to-all | bytes 4194304 | tf_op jit(solution)/shard_map/all_to_all | solution.py:18
  38.8 59.2 %all_to_all.71 = f32[32,128,128]{2,1,0:T(8,128)S(1)} all-to-all(f32[32,128,128]{2,1,0:T(8,128)S(1)} %broadcast_in_dim.25), channel_id=1, replica_groups=mesh['view'=8,'samp'=32] {'samp'}, dimensions={0} | all-to-all | bytes 4194304 | tf_op jit(solution)/shard_map/all_to_all | solution.py:18
  108.6 2.1 convolution_bitcast_fusion.6
  111.0 2.1 convolution_bitcast_fusion.7
  113.6 1.5 copy.37
  115.1 6.5 all-to-all-start.2
  121.6 46.6 %all-to-all-done.2 = f32[32,2,64,128]{3,2,1,0:T(8,128)S(1)} async-done(((f32[32,2,64,128]{3,2,1,0:T(8,128)}), f32[32,2,64,128]{3,2,1,0:T(8,128)S(1)}, u32[]{:S(2)}, u32[]{:S(2)}) %all-to-all-start.2) | async-done | bytes 2097184 | tf_op jit(solution)/shard_map/all_to_all | solution.py:33
  168.3 0.9 fusion.162
  169.4 31.2 %all_to_all.72 = bf16[32,2,64,128]{3,2,1,0:T(8,128)(2,1)S(1)} all-to-all(bf16[32,2,64,128]{3,2,1,0:T(8,128)(2,1)S(1)} %broadcast_in_dim.26), channel_id=1, replica_groups=mesh['view'=8,'samp'=32] {'samp'}, dimensions={0} | all-to-all | bytes 2097152 | tf_op jit(solution)/shard_map/all_to_all | solution.py:18
  200.8 3.8 convolution_bitcast_fusion.4
  204.9 3.8 convolution_bitcast_fusion.5
  209.6 52.6 %all_to_all.73 = f32[32,2,64,128]{3,2,1,0:T(8,128)S(1)} all-to-all(f32[32,2,64,128]{3,2,1,0:T(8,128)S(1)} %copy.42), channel_id=1, replica_groups=mesh['view'=8,'samp'=32] {'samp'}, dimensions={0} | all-to-all | bytes 4194304 | tf_op jit(solution)/shard_map/all_to_all | solution.py:33
  262.6 30.2 %all_to_all.74 = bf16[32,2,64,128]{3,2,1,0:T(8,128)(2,1)S(1)} all-to-all(bf16[32,2,64,128]{3,2,1,0:T(8,128)(2,1)S(1)} %broadcast_in_dim.27), channel_id=1, replica_groups=mesh['view'=8,'samp'=32] {'samp'}, dimensions={0} | all-to-all | bytes 2097152 | tf_op jit(solution)/shard_map/all_to_all | solution.py:18
  292.9 0.8 fusion.55
  293.7 0.8 fusion.168
  294.8 37.4 %all_to_all.75 = f32[8,512,128]{2,1,0:T(8,128)S(1)} all-to-all(f32[8,512,128]{2,1,0:T(8,128)S(1)} %broadcast_in_dim.28), channel_id=1, replica_groups=mesh['view'=8,'samp'=32] {'view'}, dimensions={0} | all-to-all | bytes 4194304 | tf_op jit(solution)/shard_map/all_to_all | solution.py:18
  333.2 53.2 %all_to_all.76 = f32[32,128,128]{2,1,0:T(8,128)S(1)} all-to-all(f32[32,128,128]{2,1,0:T(8,128)S(1)} %broadcast_in_dim.29), channel_id=1, replica_groups=mesh['view'=8,'samp'=32] {'samp'}, dimensions={0} | all-to-all | bytes 4194304 | tf_op jit(solution)/shard_map/all_to_all | solution.py:18
  397.0 2.0 convolution_bitcast_fusion.2
  399.3 2.0 convolution_bitcast_fusion.3
  402.2 53.5 %all_to_all.77 = f32[32,2,64,128]{3,2,1,0:T(8,128)S(1)} all-to-all(f32[32,2,64,128]{3,2,1,0:T(8,128)S(1)} %copy.47), channel_id=1, replica_groups=mesh['view'=8,'samp'=32] {'samp'}, dimensions={0} | all-to-all | bytes 4194304 | tf_op jit(solution)/shard_map/all_to_all | solution.py:33
  456.1 31.5 %all_to_all.78 = bf16[32,2,64,128]{3,2,1,0:T(8,128)(2,1)S(1)} all-to-all(bf16[32,2,64,128]{3,2,1,0:T(8,128)(2,1)S(1)} %broadcast_in_dim.30), channel_id=1, replica_groups=mesh['view'=8,'samp'=32] {'samp'}, dimensions={0} | all-to-all | bytes 2097152 | tf_op jit(solution)/shard_map/all_to_all | solution.py:18
  487.6 0.9 fusion.164
  488.5 3.4 convolution_bitcast_fusion
  492.3 3.6 convolution_bitcast_fusion.1
  496.7 54.0 %all_to_all.79 = f32[32,2,64,128]{3,2,1,0:T(8,128)S(1)} all-to-all(f32[32,2,64,128]{3,2,1,0:T(8,128)S(1)} %copy.50), channel_id=1, replica_groups=mesh['view'=8,'samp'=32] {'samp'}, dimensions={0} | all-to-all | bytes 4194304 | tf_op jit(solution)/shard_map/all_to_all | solution.py:33
  552.5 31.1 %all_to_all.80 = bf16[32,2,64,128]{3,2,1,0:T(8,128)(2,1)S(1)} all-to-all(bf16[32,2,64,128]{3,2,1,0:T(8,128)(2,1)S(1)} %broadcast_in_dim.31), channel_id=1, replica_groups=mesh['view'=8,'samp'=32] {'samp'}, dimensions={0} | all-to-all | bytes 2097152 | tf_op jit(solution)/shard_map/all_to_all | solution.py:18
  584.5 0.8 fusion.46
  585.6 34.9 %all_to_all.81 = f32[8,512,128]{2,1,0:T(8,128)S(1)} all-to-all(f32[8,512,128]{2,1,0:T(8,128)S(1)} %broadcast_in_dim.32), channel_id=1, replica_groups=mesh['view'=8,'samp'=32] {'view'}, dimensions={0} | all-to-all | bytes 4194304 | tf_op jit(solution)/shard_map/all_to_all | solution.py:18
  621.4 53.3 %all_to_all.82 = f32[32,128,128]{2,1,0:T(8,128)S(1)} all-to-all(f32[32,128,128]{2,1,0:T(8,128)S(1)} %broadcast_in_dim.33), channel_id=1, replica_groups=mesh['view'=8,'samp'=32] {'samp'}, dimensions={0} | all-to-all | bytes 4194304 | tf_op jit(solution)/shard_map/all_to_all | solution.py:18
  684.9 1.1 convolution_multiply_fusion
  (171 shorter events, 38.5 us)
Async XLA Ops:
  0.6 4.2 copy-start
  115.1 53.1 %all-to-all-start.2 = ((f32[32,2,64,128]{3,2,1,0:T(8,128)}), f32[32,2,64,128]{3,2,1,0:T(8,128)S(1)}, u32[]{:S(2)}, u32[]{:S(2)}) async-start(f32[32,2,64,128]{3,2,1,0:T(8,128)} %copy.37), calls=%async_computation.2 | async-start | bytes 4194304 | tf_op jit(solution)/shard_map/all_to_all | solution.py:33
  262.6 30.3 %copy-start.1 = (bf16[2,512,2048]{2,1,0:T(8,128)(2,1)S(1)}, bf16[2,512,2048]{2,1,0:T(8,128)(2,1)}, u32[]{:S(2)}) copy-start(bf16[2,512,2048]{2,1,0:T(8,128)(2,1)} %param.2) | copy-start | bytes 12582916
  455.8 32.7 %copy-start.3 = (f32[2,64,128]{2,1,0:T(8,128)}, f32[2,64,128]{2,1,0:T(8,128)S(1)}, u32[]{:S(2)}) copy-start(f32[2,64,128]{2,1,0:T(8,128)S(1)} %reduce_sum.149) | copy-start | bytes 196612
  550.7 0.8 copy-start.4
  552.5 31.2 %copy-start.2 = (bf16[2,512,2048]{2,1,0:T(8,128)(2,1)S(1)}, bf16[2,512,2048]{2,1,0:T(8,128)(2,1)}, u32[]{:S(2)}) copy-start(bf16[2,512,2048]{2,1,0:T(8,128)(2,1)} %param.2) | copy-start | bytes 12582916
where the time goes:
time: 689 us; the launch traced here: 686 us
  blocking collectives  554 us (80%)
  matrix products  54.1 us (8%)
  waiting for transfers between devices  46.6 us (7%)
  other arithmetic  9.28 us (1%)
  local copies, waits for them, and re-layouts  8.97 us (1%)
    all_to_all x10, blocking collectives, copy_for_each(): lax.all_to_all(jnp.broadcast_to(x[None], (peers, *x.shape)), axis, 0, 0,...  394 us
    all_to_all x3, blocking collectives, sent_and_summed(): parts = lax.all_to_all(split_up(x, dim, peers), axis, 0, 0, tiled=True)  160 us
    all_to_all x1, waiting for transfers between devices, sent_and_summed(): parts = lax.all_to_all(split_up(x, dim, peers), axis, 0, 0, tiled=True)  46.6 us
    dot_general x8, matrix products, grad_term(): lax.dot_general(samples, resid, (((0,), (0,)), ((), ())), preferred_eleme...  22.8 us
  transfers between devices with their start and end apart: 1, of which 1 were waited for; matrix products, arithmetic and copies ran while one was open for 0% of the time, Pallas kernels for 0%

commit v1 on v0

v1 whole, which is shorter than its diff:
```python
import functools

import jax
import jax.numpy as jnp
from jax import lax
from jax.experimental import pallas as pl
from jax.experimental.pallas import tpu as pltpu
from jax.sharding import PartitionSpec as P

OUTER = 2
NS_ITERS = 12
RIDGE = 0.1
STEP = 0.5

HIGH = lax.Precision.HIGHEST
MESH = pl.DeviceIdType.MESH
F32 = jnp.float32
BF16 = jnp.bfloat16

NX, NC, NY, NZ = 4, 2, 4, 8
VIEWS, ROWS, FEATS, K = 2, 512, 2048, 128
BLOCK = FEATS // NZ
OWN = BLOCK // NY
MAIN, REST = 48, 16
SAMPLES = ROWS * NY * NZ
GROWS = K // (NX * NC)
SROWS = ROWS // (NX * NC)


def dot32(a, b):
    return jnp.dot(a, b, precision=HIGH, preferred_element_type=F32)


def dot16(a, b):
    return jnp.dot(a, b, preferred_element_type=F32)


def far_first(i):
    odd = lax.rem(i, 2)
    return lax.rem(4 + odd * ((i + 1) // 2) - (1 - odd) * (i // 2), NZ)


def kernel(
    x_ref, w_ref, scores_ref, coeffs_ref,
    xt, wb, gb, p, pb, sb, wrow, bm, ga,
    vloc, vin, summed, gram, gpart, gyin, gzout, gzin,
    ryin, szout, rz2in, rz1in, syout, ry2in,
    vrs_s, vrs_r, vag_s, vag_r, gy_s, gy_r, gz_s, gz_r, gv_s, gv_r,
    ry_s, ry_r, rz2_s, rz2_r, rz1_s, rz1_r, ry2_s, ry2_r,
    az_s, az_r, ayf_s, ayf_r, ay_s, ay_r, az2_s, az2_r,
):
    v = lax.axis_index("view")
    s = lax.axis_index("samp")
    y, z = lax.rem(s, NY), s // NY

    def y_peer(m):
        return {"view": v, "samp": z * NY + lax.rem(y + m, NY)}

    def z_peer(j):
        return {"view": v, "samp": lax.rem(z + j, NZ) * NY + y}

    def v_peer(j):
        return {"view": lax.rem(v + j, NX * NC), "samp": s}

    def copy(src, dst, send, recv, device):
        return pltpu.make_async_remote_copy(
            src_ref=src, dst_ref=dst, send_sem=send, recv_sem=recv, device_id=device, device_id_type=MESH
        )

    barrier = pltpu.get_barrier_semaphore()
    for m in range(1, NY):
        pl.semaphore_signal(barrier, inc=1, device_id=y_peer(m), device_id_type=MESH)
    for j in range(1, NZ):
        pl.semaphore_signal(barrier, inc=1, device_id=z_peer(j), device_id_type=MESH)
    for j in range(1, NX * NC):
        pl.semaphore_signal(barrier, inc=1, device_id=v_peer(j), device_id_type=MESH)

    def vrs_copy(t, j):
        to = lax.rem(v + j, NX * NC)
        return copy(vloc.at[t, to], vin.at[t, j], vrs_s.at[t, j], vrs_r.at[t, j], v_peer(j))

    def vag_copy(t, j):
        block = summed.at[t, pl.ds(v * SROWS, SROWS)]
        return copy(block, block, vag_s.at[t, j], vag_r.at[t, j], v_peer(j))

    def vrs_start(t):
        vloc[t] = (p[0] + p[1]).reshape(NX * NC, SROWS, K).astype(vloc.dtype)
        for j in range(1, NX * NC):
            vrs_copy(t, j).start()

    def vrs_end(t):
        total = vloc[t, v].astype(F32)
        for j in range(1, NX * NC):
            vrs_copy(t, j).wait()
            total = total + vin[t, j].astype(F32)
        summed[t, pl.ds(v * SROWS, SROWS)] = total
        for j in range(1, NX * NC):
            vag_copy(t, j).start()

    def vag_end(t):
        for j in range(1, NX * NC):
            vag_copy(t, j).wait()

    def gy_copy(t, m):
        return copy(gpart.at[t, v], gyin.at[t, m], gy_s.at[t, m], gy_r.at[t, m], y_peer(m))

    def gz_copy(t, j):
        return copy(gzout.at[t], gzin.at[t, j], gz_s.at[t, j], gz_r.at[t, j], z_peer(j))

    def gv_copy(t, j):
        block = gram.at[t, pl.ds(v * GROWS, GROWS)]
        return copy(block, block, gv_s.at[t, j], gv_r.at[t, j], v_peer(j))

    def gram_start(t):
        everyone = summed[t]
        gpart[t] = dot32(everyone.T, everyone).reshape(NX * NC, GROWS, K)
        for m in range(1, NY):
            gy_copy(t, m).start()

    def gram_y_end(t):
        total = gpart[t, v]
        for m in range(1, NY):
            gy_copy(t, m).wait()
            total = total + gyin[t, m]
        gzout[t] = total
        for j in range(1, NZ):
            gz_copy(t, j).start()

    def gram_z_end(t):
        total = gzout[t]
        for j in range(1, NZ):
            gz_copy(t, j).wait()
            total = total + gzin[t, j]
        gram[t, pl.ds(v * GROWS, GROWS)] = total
        for j in range(1, NX * NC):
            gv_copy(t, j).start()

    def gram_end(t):
        for j in range(1, NX * NC):
            gv_copy(t, j).wait()

    def eye_mat():
        row = lax.broadcasted_iota(jnp.int32, (K, K), 0)
        col = lax.broadcasted_iota(jnp.int32, (K, K), 1)
        return jnp.where(row == col, 1.0, 0.0).astype(F32)

    def newton_init(t):
        eye = eye_mat()
        full = gram[t]
        trace = jnp.sum(full * eye, keepdims=True)
        shrunk = full + trace / K * eye
        scale = jnp.sqrt(jnp.sum(shrunk * shrunk, keepdims=True))
        return shrunk / scale, eye, scale

    def newton_turns(approx, inverse, turns):
        eye = eye_mat()

        def turn(_, both):
            approx, inverse = both[:, :K], both[:, K:]
            factor = 0.5 * (3.0 * eye - dot32(inverse, approx))
            return dot32(factor, both)

        both = lax.fori_loop(0, turns, turn, jnp.concatenate([approx, inverse], axis=1))
        return both[:, :K], both[:, K:]

    def ry_copy(r, j, m):
        to_z, to_y = lax.rem(z + j, NZ), lax.rem(y + m, NY)
        return copy(
            gb.at[r, :, to_z, to_y, pl.ds(0, MAIN)], ryin.at[r, j, m], ry_s.at[r, j, m], ry_r.at[r, j, m], y_peer(m)
        )

    def rz1_copy(r, j):
        to_z = lax.rem(z + j, NZ)
        return copy(
            gb.at[r, :, to_z, :, pl.ds(MAIN, REST)], rz1in.at[r, j], rz1_s.at[r, j], rz1_r.at[r, j], z_peer(j)
        )

    def rz2_copy(r, j):
        return copy(szout.at[r, j], rz2in.at[r, j], rz2_s.at[r, j], rz2_r.at[r, j], z_peer(j))

    def ry2_copy(r, m):
        to_y = lax.rem(y + m, NY)
        return copy(syout.at[r, to_y], ry2in.at[r, m], ry2_s.at[r, m], ry2_r.at[r, m], y_peer(m))

    def rs_start(r, right):
        def step(i, _):
            j = far_first(i)
            to_z = lax.rem(z + j, NZ)
            rows = pl.ds(pl.multiple_of(to_z * BLOCK, BLOCK), BLOCK)
            for member in range(VIEWS):
                block = dot16(xt[member, rows, :], right(member))
                gb[r, member, to_z] = block.astype(BF16).reshape(NY, OWN, K)
            for m in range(1, NY):
                ry_copy(r, j, m).start()

            @pl.when(i < NZ - 1)
            def _():
                rz1_copy(r, j).start()

            return 0

        lax.fori_loop(0, NZ, step, 0)

    def rs_mid(r):
        def step(i, _):
            j = far_first(i)
            to_z = lax.rem(z + j, NZ)
            total = gb[r, :, to_z, y, 0:MAIN].astype(F32)
            for m in range(1, NY):
                ry_copy(r, j, m).wait()
                total = total + ryin[r, j, m].astype(F32)
            szout[r, j] = total.astype(BF16)

            @pl.when(i < NZ - 1)
            def _():
                rz2_copy(r, j).start()

            return 0

        lax.fori_loop(0, NZ, step, 0)
        total = gb[r, :, z, :, MAIN:OWN].astype(F32)
        for j in range(1, NZ):
            rz1_copy(r, j).wait()
            total = total + rz1in[r, j].astype(F32)
        for to in range(NY):
            syout[r, to] = total[:, to].astype(BF16)
        for m in range(1, NY):
            ry2_copy(r, m).start()

    def rs_end(r):
        total = syout[r, y].astype(F32)
        for m in range(1, NY):
            ry2_copy(r, m).wait()
            total = total + ry2in[r, m].astype(F32)
        ga[:, MAIN:OWN] = total
        total = szout[r, 0].astype(F32)
        for j in range(1, NZ):
            rz2_copy(r, j).wait()
            total = total + rz2in[r, j].astype(F32)
        ga[:, 0:MAIN] = total

    def az_copy(a, j):
        block = wb.at[a, :, z, y, pl.ds(0, MAIN)]
        return copy(block, block, az_s.at[a, j], az_r.at[a, j], z_peer(j))

    def ayf_copy(a, j, m):
        from_z = lax.rem(z - j + NZ, NZ)
        block = wb.at[a, :, from_z, y, pl.ds(0, MAIN)]
        return copy(block, block, ayf_s.at[a, j, m], ayf_r.at[a, j, m], y_peer(m))

    def ay_copy(a, m):
        block = wb.at[a, :, z, y, pl.ds(MAIN, REST)]
        return copy(block, block, ay_s.at[a, m], ay_r.at[a, m], y_peer(m))

    def az2_copy(a, j):
        block = wb.at[a, :, z, :, pl.ds(MAIN, REST)]
        return copy(block, block, az2_s.at[a, j], az2_r.at[a, j], z_peer(j))

    def gather_start(a):
        wb[a, :, z, y] = wrow[...].astype(BF16)
        for m in range(1, NY):
            ay_copy(a, m).start()
        for j in (1, 7, 2, 6, 3, 5, 4):
            az_copy(a, j).start()
        for m in range(1, NY):
            ayf_copy(a, 0, m).start()

    def gather_products(a):
        for m in range(1, NY):
            ay_copy(a, m).wait()
        for j in (4, 5, 3, 6, 2, 7, 1):
            az2_copy(a, j).start()

        def forward(i, _):
            j = far_first(NZ - 1 - i)
            az_copy(a, j).wait()
            for m in range(1, NY):
                ayf_copy(a, j, m).start()
            return 0

        lax.fori_loop(1, NZ, forward, 0)

        p[...] = jnp.zeros_like(p)

        def product(i, _):
            j = far_first(NZ - 1 - i)
            from_z = lax.rem(z - j + NZ, NZ)
            for m in range(1, NY):
                ayf_copy(a, j, m).wait()

            @pl.when(i > 0)
            def _():
                az2_copy(a, j).wait()

            product_of(a, from_z)
            return 0

        lax.fori_loop(0, NZ, product, 0)

    def product_of(a, from_z):
        cols = pl.ds(pl.multiple_of(from_z * BLOCK, BLOCK), BLOCK)
        for member in range(VIEWS):
            p[member] += dot16(x_ref[member, :, cols], wb[a, member, from_z].reshape(BLOCK, K))

    def update():
        grad = (ga[...].reshape(VIEWS * OWN, K) - bm[...]) / SAMPLES
        old = wrow[...].reshape(VIEWS * OWN, K)
        wrow[...] = (old - STEP * (grad + RIDGE * old)).reshape(VIEWS, OWN, K)

    wb[0] = w_ref[...].reshape(VIEWS, NZ, NY, OWN, K).astype(BF16)
    wrow[...] = w_ref[:, pl.ds(pl.multiple_of(s * OWN, OWN), OWN), :]
    p[...] = jnp.zeros_like(p)

    def first(i, _):
        product_of(0, i)
        return 0

    lax.fori_loop(0, NZ, first, 0)
    pl.semaphore_wait(barrier, (NY - 1) + (NZ - 1) + (NX * NC - 1))

    def turn_over(i, _):
        cols = pl.ds(pl.multiple_of(i * BLOCK, BLOCK), BLOCK)
        for member in range(VIEWS):
            xt[member, cols, :] = x_ref[member, :, cols].T
        return 0

    lax.fori_loop(0, NZ, turn_over, 0)

    def outer(o, _):
        own_r, sum_r, next_r = 3 * o, 3 * o + 1, 3 * o + 2
        vrs_start(o)
        pb[...] = p[...].astype(BF16)
        rs_start(own_r, lambda member: pb[member])
        vrs_end(o)
        vag_end(o)
        gram_start(o)
        sb[...] = summed[o].astype(BF16)
        gram_y_end(o)
        rs_mid(own_r)
        rs_start(sum_r, lambda member: sb[...])
        gram_z_end(o)
        rs_end(own_r)
        gram_end(o)
        approx, inverse, scale = newton_init(o)
        approx, inverse = newton_turns(approx, inverse, NS_ITERS // 2)
        rs_mid(sum_r)
        approx, inverse = newton_turns(approx, inverse, NS_ITERS - NS_ITERS // 2)
        white = inverse * jnp.sqrt(SAMPLES / scale)
        grad_own = ga[...]
        rs_end(sum_r)
        bm[...] = dot32(ga[...].reshape(VIEWS * OWN, K), white)
        ga[...] = grad_own
        update()
        gather_start(2 * o + 1)
        gather_products(2 * o + 1)
        pb[...] = p[...].astype(BF16)
        rs_start(next_r, lambda member: pb[member])
        rs_mid(next_r)
        rs_end(next_r)
        update()
        gather_start(2 * o + 2)
        gather_products(2 * o + 2)
        return 0

    lax.fori_loop(0, OUTER, outer, 0)
    vrs_start(OUTER)
    coeffs_ref[...] = wrow[...]
    vrs_end(OUTER)
    vag_end(OUTER)
    gram_start(OUTER)
    gram_y_end(OUTER)
    gram_z_end(OUTER)
    gram_end(OUTER)
    approx, inverse, scale = newton_init(OUTER)
    approx, inverse = newton_turns(approx, inverse, NS_ITERS)
    scores_ref[...] = dot32(summed[OUTER], inverse * jnp.sqrt(SAMPLES / scale))


def body(view_data, init_coeffs):
    evals, reduces, gathers = OUTER + 1, 3 * OUTER, 2 * OUTER
    peers = NX * NC
    vmem, dma = pltpu.VMEM, pltpu.SemaphoreType.DMA
    scratch = [
        vmem((VIEWS, FEATS, ROWS), BF16),
        vmem((gathers + 1, VIEWS, NZ, NY, OWN, K), BF16),
        vmem((reduces, VIEWS, NZ, NY, OWN, K), BF16),
        vmem((VIEWS, ROWS, K), F32),
        vmem((VIEWS, ROWS, K), BF16),
        vmem((ROWS, K), BF16),
        vmem((VIEWS, OWN, K), F32),
        vmem((VIEWS * OWN, K), F32),
        vmem((VIEWS, OWN, K), F32),
        vmem((evals, peers, SROWS, K), BF16),
        vmem((evals, peers, SROWS, K), BF16),
        vmem((evals, ROWS, K), F32),
        vmem((evals, K, K), F32),
        vmem((evals, peers, GROWS, K), F32),
        vmem((evals, NY, GROWS, K), F32),
        vmem((evals, GROWS, K), F32),
        vmem((evals, NZ, GROWS, K), F32),
        vmem((reduces, NZ, NY, VIEWS, MAIN, K), BF16),
        vmem((reduces, NZ, VIEWS, MAIN, K), BF16),
        vmem((reduces, NZ, VIEWS, MAIN, K), BF16),
        vmem((reduces, NZ, VIEWS, NY, REST, K), BF16),
        vmem((reduces, NY, VIEWS, REST, K), BF16),
        vmem((reduces, NY, VIEWS, REST, K), BF16),
    ]
    for shape in (
        (evals, peers), (evals, peers), (evals, NY), (evals, NZ), (evals, peers),
        (reduces, NZ, NY), (reduces, NZ), (reduces, NZ), (reduces, NY),
        (gathers + 1, NZ), (gathers + 1, NZ, NY), (gathers + 1, NY), (gathers + 1, NZ),
    ):
        scratch += [dma(shape), dma(shape)]
    return pl.pallas_call(
        kernel,
        out_shape=(jax.ShapeDtypeStruct((ROWS, K), F32), jax.ShapeDtypeStruct((VIEWS, OWN, K), F32)),
        in_specs=[pl.BlockSpec(memory_space=pltpu.VMEM)] * 2,
        out_specs=(pl.BlockSpec(memory_space=pltpu.VMEM),) * 2,
        scratch_shapes=scratch,
        compiler_params=pltpu.CompilerParams(collective_id=0, has_side_effects=True, vmem_limit_bytes=56 << 20),
        name="gcca",
    )(view_data, init_coeffs)


def solution(mesh):
    in_specs = (P("view", "samp", None), P("view", None, None))
    out_specs = (P("samp", None), P("view", "samp", None))
    return jax.shard_map(body, mesh=mesh, in_specs=in_specs, out_specs=out_specs, check_vma=False)
```

time: 689 us -> 213 us (0.31)
  blocking collectives: 554 us -> 0 us
  Pallas kernels: 0 us -> 209 us
  matrix products: 54.1 us -> 0 us
  waiting for transfers between devices: 46.6 us -> 0 us
  other arithmetic: 9.28 us -> 0 us
    all_to_all x13 -> x0, blocking collectives: 554 us -> none  [the longest x10 394 us: copy_for_each(): lax.all_to_all(jnp.broadcast_to(x[None], (peers, *x.shape)), axis, 0, 0,...]
    pallas_call x0 -> x1, Pallas kernels: none -> 209 us  [body(): pl.pallas_call(kernel, out_shape=(jax.ShapeDtypeStruct((ROWS, K), F32), j...]
    dot_general x125 -> x0, matrix products: 54.1 us -> none  [the longest x8 22.8 us: grad_term(): lax.dot_general(samples, resid, (((0,), (0,)), ((), ())), preferred_eleme...]
    all_to_all x1 -> x0, waiting for transfers between devices: 46.6 us -> none  [sent_and_summed(): parts = lax.all_to_all(split_up(x, dim, peers), axis, 0, 0, tiled=True)]
  transfers between devices with their start and end apart: 1 -> 0, of which waited for: 1 -> 0; matrix products, arithmetic and copies ran while one was open for 0% -> 0% of each run, Pallas kernels for 0% -> 0%
where the time goes in v1:
time: 213 us
  Pallas kernels  209 us (98%)
  local copies, waits for them, and re-layouts  3.14 us (1%)
    pallas_call x1, Pallas kernels, body(): pl.pallas_call(kernel, out_shape=(jax.ShapeDtypeStruct((ROWS, K), F32), j...  209 us

profile of v1, /device:TPU:1, one launch (start us, length us, event | category | flops | bytes accessed | tf_op | source)
XLA Modules:
  0.0 212.9 jit_solution(13205647059152256582)
XLA Ops:
  0.6 209.1 %gcca.1 = (f32[512,128]{1,0:T(8,128)}, f32[2,64,128]{2,1,0:T(8,128)}) custom-call(bf16[2,512,2048]{2,1,0:T(8,128)(2,1)} %x_ref.1, f32[2,2048,128]{2,1,0:T(8,128)} %w_ref.1), custom_call_target="tpu_custom_call" | custom-call | tf_op jit(solution)/shard_map/gcca/pallas_call | solution.py:414
  209.7 1.7 copy.6
  211.4 1.5 copy.7

commit v2 on v1

v2 whole, which is shorter than its diff:
```python
import functools

import jax
import jax.numpy as jnp
from jax import lax
from jax.experimental import pallas as pl
from jax.experimental.pallas import tpu as pltpu
from jax.sharding import PartitionSpec as P

OUTER = 2
NS_ITERS = 12
RIDGE = 0.1
STEP = 0.5

HIGH = lax.Precision.HIGHEST
MESH = pl.DeviceIdType.MESH
F32 = jnp.float32
BF16 = jnp.bfloat16

NX, NC, NY, NZ = 4, 2, 4, 8
VIEWS, ROWS, FEATS, K = 2, 512, 2048, 128
BLOCK = FEATS // NZ
OWN = BLOCK // NY
MAIN, REST = 48, 16
SAMPLES = ROWS * NY * NZ
PEERS = NX * NC
SENT = (NY * NZ - 1) * OWN * K // ROWS
GROWS = K // (NX * NC)
SROWS = ROWS // (NX * NC)


def dot32(a, b):
    return jnp.dot(a, b, precision=HIGH, preferred_element_type=F32)


def dot16(a, b):
    return jnp.dot(a, b, preferred_element_type=F32)


def far_first(i):
    odd = lax.rem(i, 2)
    return lax.rem(4 + odd * ((i + 1) // 2) - (1 - odd) * (i // 2), NZ)


def kernel(
    x_ref, w_ref, scores_ref, coeffs_ref,
    xt, wb, gb, p, pb, sb, wrow, bm, ga, gs,
    vloc, vin, summed, gram, gpart, gvin, gyout, gyin, gzout, gzin,
    ryin, szout, rz2in, rz1in, syout, ry2in,
    vrs_r, vag_r, gx_r, gy_r, gz_r, gv_r, vrs_s, vag_s, gram_s,
    ry_r, rz2_r, rz1_r, ry2_r, rs_s,
    az_r, ayf_r, ay_r, az2_r, ag_s,
):
    v = lax.axis_index("view")
    s = lax.axis_index("samp")
    y, z = lax.rem(s, NY), s // NY

    def y_peer(m):
        return {"view": v, "samp": z * NY + lax.rem(y + m, NY)}

    def z_peer(j):
        return {"view": v, "samp": lax.rem(z + j, NZ) * NY + y}

    def v_peer(j):
        return {"view": lax.rem(v + j, PEERS), "samp": s}

    def copy(src, dst, send, recv, device):
        return pltpu.make_async_remote_copy(
            src_ref=src, dst_ref=dst, send_sem=send, recv_sem=recv, device_id=device, device_id_type=MESH
        )

    def arrived(ref, recv):
        copy(ref, ref, ag_s.at[0], recv, y_peer(1)).wait_recv()

    def sent(ref, send):
        copy(ref, ref, send, ay_r.at[0], y_peer(1)).wait_send()

    barrier = pltpu.get_barrier_semaphore()
    for m in range(1, NY):
        pl.semaphore_signal(barrier, inc=1, device_id=y_peer(m), device_id_type=MESH)
    for j in range(1, NZ):
        pl.semaphore_signal(barrier, inc=1, device_id=z_peer(j), device_id_type=MESH)
    for j in range(1, PEERS):
        pl.semaphore_signal(barrier, inc=1, device_id=v_peer(j), device_id_type=MESH)

    def vrs_start(t):
        vloc[t] = (p[0] + p[1]).reshape(PEERS, SROWS, K).astype(vloc.dtype)
        for j in range(1, PEERS):
            to = lax.rem(v + j, PEERS)
            copy(vloc.at[t, to], vin.at[t, j], vrs_s.at[0], vrs_r.at[0], v_peer(j)).start()

    def vrs_end(t):
        total = vloc[t, v].astype(F32)
        arrived(vin.at[t, pl.ds(1, PEERS - 1)], vrs_r.at[0])
        for j in range(1, PEERS):
            total = total + vin[t, j].astype(F32)
        summed[t, pl.ds(v * SROWS, SROWS)] = total
        gpart[t] = dot32(total.T, total).reshape(PEERS, GROWS, K)
        for j in range(1, PEERS):
            to = lax.rem(v + j, PEERS)
            copy(gpart.at[t, to], gvin.at[t, j], gram_s.at[0], gx_r.at[0], v_peer(j)).start()
        block = summed.at[t, pl.ds(v * SROWS, SROWS)]
        for j in range(1, PEERS):
            copy(block, block, vag_s.at[0], vag_r.at[0], v_peer(j)).start()

    def vag_end(t):
        arrived(summed.at[t, pl.ds(0, ROWS - SROWS)], vag_r.at[0])

    def gram_v_end(t):
        total = gpart[t, v]
        arrived(gvin.at[t, pl.ds(1, PEERS - 1)], gx_r.at[0])
        for j in range(1, PEERS):
            total = total + gvin[t, j]
        gyout[t] = total
        for m in range(1, NY):
            copy(gyout.at[t], gyin.at[t, m], gram_s.at[0], gy_r.at[0], y_peer(m)).start()

    def gram_y_end(t):
        total = gyout[t]
        arrived(gyin.at[t, pl.ds(1, NY - 1)], gy_r.at[0])
        for m in range(1, NY):
            total = total + gyin[t, m]
        gzout[t] = total
        for j in (4, 5, 3, 6, 2, 7, 1):
            copy(gzout.at[t], gzin.at[t, j], gram_s.at[0], gz_r.at[0], z_peer(j)).start()

    def gram_z_end(t):
        total = gzout[t]
        arrived(gzin.at[t, pl.ds(1, NZ - 1)], gz_r.at[0])
        for j in range(1, NZ):
            total = total + gzin[t, j]
        gram[t, pl.ds(v * GROWS, GROWS)] = total
        block = gram.at[t, pl.ds(v * GROWS, GROWS)]
        for j in range(1, PEERS):
            copy(block, block, gram_s.at[0], gv_r.at[0], v_peer(j)).start()

    def gram_end(t):
        arrived(gram.at[t, pl.ds(0, K - GROWS)], gv_r.at[0])
        sent(vin.at[t, pl.ds(1, PEERS - 1)], vrs_s.at[0])
        sent(summed.at[t, pl.ds(0, ROWS - SROWS)], vag_s.at[0])
        sent(summed.at[t, pl.ds(0, (3 * 7 + 3) * GROWS)], gram_s.at[0])

    def eye_mat():
        row = lax.broadcasted_iota(jnp.int32, (K, K), 0)
        col = lax.broadcasted_iota(jnp.int32, (K, K), 1)
        return jnp.where(row == col, 1.0, 0.0).astype(F32)

    def newton_init(t):
        eye = eye_mat()
        full = gram[t]
        trace = jnp.sum(full * eye, keepdims=True)
        shrunk = full + trace / K * eye
        scale = jnp.sqrt(jnp.sum(shrunk * shrunk, keepdims=True))
        return jnp.concatenate([shrunk / scale, eye], axis=1), scale

    def newton_turns(first, last, both, beside=None):
        eye = eye_mat()

        def turn(i, both):
            approx, inverse = both[:, :K], both[:, K:]
            factor = 0.5 * (3.0 * eye - dot32(inverse, approx))
            both = dot32(factor, both)
            if beside is not None:
                beside(i)
            return both

        return lax.fori_loop(first, last, turn, both)

    def ry_start(r, q, member, j):
        to_z = lax.rem(z + j, NZ)
        for m in range(1, NY):
            to_y = lax.rem(y + m, NY)
            copy(
                gb.at[r, member, to_z, to_y, pl.ds(0, MAIN)], ryin.at[r, member, j, m],
                rs_s.at[q, member], ry_r.at[q, member, j], y_peer(m),
            ).start()

    def rz1_start(r, q, member, j):
        to_z = lax.rem(z + j, NZ)
        copy(
            gb.at[r, member, to_z, :, pl.ds(MAIN, REST)], rz1in.at[r, member, j],
            rs_s.at[q, member], rz1_r.at[q, member], z_peer(j),
        ).start()

    def rs_start(r, q, member, right, both_orders=True):
        def step(i, _):
            j = far_first(i)
            to_z = lax.rem(z + j, NZ)
            rows = pl.ds(pl.multiple_of(to_z * BLOCK, BLOCK), BLOCK)
            block = dot16(xt[member, rows, :], right())
            gb[r, member, to_z] = block.astype(BF16).reshape(NY, OWN, K)
            ry_start(r, q, member, j)
            if both_orders:

                @pl.when(i < NZ - 1)
                def _():
                    rz1_start(r, q, member, j)

            return 0

        lax.fori_loop(0, NZ, step, 0)

    def rs_other_order(r, q, member):
        for j in (4, 5, 3, 6, 2, 7, 1):
            rz1_start(r, q, member, j)

    def rs_mid_step(r, q, member, i):
        j = far_first(i)
        to_z = lax.rem(z + j, NZ)
        total = gb[r, member, to_z, y, 0:MAIN].astype(F32)
        arrived(ryin.at[r, member, j, pl.ds(1, NY - 1)], ry_r.at[q, member, j])
        for m in range(1, NY):
            total = total + ryin[r, member, j, m].astype(F32)
        szout[r, member, j] = total.astype(BF16)

        @pl.when(i < NZ - 1)
        def _():
            copy(
                szout.at[r, member, j], rz2in.at[r, member, j], rs_s.at[q, member], rz2_r.at[q, member], z_peer(j)
            ).start()

    def rs_mid_rest(r, q, member):
        total = gb[r, member, z, :, MAIN:OWN].astype(F32)
        arrived(rz1in.at[r, member, pl.ds(1, NZ - 1)], rz1_r.at[q, member])
        for j in range(1, NZ):
            total = total + rz1in[r, member, j].astype(F32)
        syout[r, member] = total.astype(BF16)
        for m in range(1, NY):
            to_y = lax.rem(y + m, NY)
            copy(
                syout.at[r, member, to_y], ry2in.at[r, member, m], rs_s.at[q, member], ry2_r.at[q, member], y_peer(m)
            ).start()

    def rs_mid(r, q, member):
        def step(i, _):
            rs_mid_step(r, q, member, i)
            return 0

        lax.fori_loop(0, NZ, step, 0)
        rs_mid_rest(r, q, member)

    def rs_end(r, q, member, out):
        total = syout[r, member, y].astype(F32)
        arrived(ry2in.at[r, member, pl.ds(1, NY - 1)], ry2_r.at[q, member])
        for m in range(1, NY):
            total = total + ry2in[r, member, m].astype(F32)
        out[member, MAIN:OWN] = total
        total = szout[r, member, 0].astype(F32)
        arrived(rz2in.at[r, member, pl.ds(1, NZ - 1)], rz2_r.at[q, member])
        for j in range(1, NZ):
            total = total + rz2in[r, member, j].astype(F32)
        out[member, 0:MAIN] = total
        sent(xt.at[0, pl.ds(0, SENT)], rs_s.at[q, member])

    def ayf_start(a, member, j):
        from_z = lax.rem(z - j + NZ, NZ)
        block = wb.at[a, member, from_z, y, pl.ds(0, MAIN)]
        for m in range(1, NY):
            copy(block, block, ag_s.at[member], ayf_r.at[member, j], y_peer(m)).start()

    def gather_start(a, member):
        wb[a, member, z, y] = wrow[member].astype(BF16)
        block = wb.at[a, member, z, y, pl.ds(MAIN, REST)]
        for m in range(1, NY):
            copy(block, block, ag_s.at[member], ay_r.at[member], y_peer(m)).start()
        block = wb.at[a, member, z, y, pl.ds(0, MAIN)]
        for j in (1, 7, 2, 6, 3, 5, 4):
            copy(block, block, ag_s.at[member], az_r.at[member, j], z_peer(j)).start()
        ayf_start(a, member, 0)

    def gather_forward(a, member):
        arrived(wb.at[a, member, z, pl.ds(0, NY - 1), pl.ds(0, REST)], ay_r.at[member])
        block = wb.at[a, member, z, :, pl.ds(MAIN, REST)]
        for j in (4, 5, 3, 6, 2, 7, 1):
            copy(block, block, ag_s.at[member], az2_r.at[member, j], z_peer(j)).start()

        def forward(i, _):
            j = far_first(NZ - 1 - i)
            arrived(wb.at[a, member, z, y, pl.ds(0, MAIN)], az_r.at[member, j])
            ayf_start(a, member, j)
            return 0

        lax.fori_loop(1, NZ, forward, 0)

    def gather_products(a, member):
        p[member] = jnp.zeros((ROWS, K), F32)

        def product(i, _):
            j = far_first(NZ - 1 - i)
            from_z = lax.rem(z - j + NZ, NZ)
            arrived(wb.at[a, member, z, pl.ds(0, NY - 1), pl.ds(0, MAIN)], ayf_r.at[member, j])

            @pl.when(i > 0)
            def _():
                arrived(wb.at[a, member, z, :, pl.ds(0, REST)], az2_r.at[member, j])

            product_of(a, member, from_z)
            return 0

        lax.fori_loop(0, NZ, product, 0)
        sent(xt.at[0, pl.ds(0, SENT)], ag_s.at[member])

    def product_of(a, member, from_z):
        cols = pl.ds(pl.multiple_of(from_z * BLOCK, BLOCK), BLOCK)
        p[member] += dot16(x_ref[member, :, cols], wb[a, member, from_z].reshape(BLOCK, K))

    def update(member):
        grad = (ga[member] - bm[member]) / SAMPLES
        wrow[member] = wrow[member] - STEP * (grad + RIDGE * wrow[member])

    wb[0] = w_ref[...].reshape(VIEWS, NZ, NY, OWN, K).astype(BF16)
    wrow[...] = w_ref[:, pl.ds(pl.multiple_of(s * OWN, OWN), OWN), :]
    p[...] = jnp.zeros_like(p)

    def first(i, _):
        cols = pl.ds(pl.multiple_of(i * BLOCK, BLOCK), BLOCK)
        for member in range(VIEWS):
            product_of(0, member, i)
            xt[member, cols, :] = x_ref[member, :, cols].T
        return 0

    lax.fori_loop(0, NZ, first, 0)
    pl.semaphore_wait(barrier, (NY - 1) + (NZ - 1) + (PEERS - 1))

    def outer(o, _):
        own_r, sum_r, next_r = 3 * o, 3 * o + 1, 3 * o + 2
        one, two = 2 * o + 1, 2 * o + 2
        vrs_start(o)
        for member in range(VIEWS):
            pb[member] = p[member].astype(BF16)
            rs_start(own_r, 0, member, lambda: pb[member])
        vrs_end(o)
        gram_v_end(o)
        vag_end(o)
        sb[...] = summed[o].astype(BF16)
        for member in range(VIEWS):
            rs_start(sum_r, 1, member, lambda: sb[...], both_orders=False)
        gram_y_end(o)
        for member in range(VIEWS):
            rs_mid(own_r, 0, member)
        for member in range(VIEWS):
            rs_other_order(sum_r, 1, member)
        gram_z_end(o)
        for member in range(VIEWS):
            rs_end(own_r, 0, member, ga)
        gram_end(o)
        both, scale = newton_init(o)

        def beside(i):
            for member in range(VIEWS):
                rs_mid_step(sum_r, 1, member, i)

        both = newton_turns(0, NZ, both, beside)
        for member in range(VIEWS):
            rs_mid_rest(sum_r, 1, member)
        both = newton_turns(NZ, NS_ITERS, both)
        white = both[:, K:] * jnp.sqrt(SAMPLES / scale)
        for member in range(VIEWS):
            rs_end(sum_r, 1, member, gs)
            bm[member] = dot32(gs[member], white)
            update(member)
            gather_start(one, member)
        for member in range(VIEWS):
            gather_forward(one, member)
        for member in range(VIEWS):
            gather_products(one, member)
            pb[member] = p[member].astype(BF16)
            rs_start(next_r, 0, member, lambda: pb[member])
        for member in range(VIEWS):
            rs_mid(next_r, 0, member)
        for member in range(VIEWS):
            rs_end(next_r, 0, member, ga)
            update(member)
            gather_start(two, member)
        for member in range(VIEWS):
            gather_forward(two, member)
        for member in range(VIEWS):
            gather_products(two, member)
        return 0

    lax.fori_loop(0, OUTER, outer, 0)
    vrs_start(OUTER)
    coeffs_ref[...] = wrow[...]
    vrs_end(OUTER)
    gram_v_end(OUTER)
    gram_y_end(OUTER)
    gram_z_end(OUTER)
    vag_end(OUTER)
    gram_end(OUTER)
    both, scale = newton_init(OUTER)
    both = newton_turns(0, NS_ITERS, both)
    scores_ref[...] = dot32(summed[OUTER], both[:, K:] * jnp.sqrt(SAMPLES / scale))


def body(view_data, init_coeffs):
    evals, reduces, gathers = OUTER + 1, 3 * OUTER, 2 * OUTER
    vmem, dma = pltpu.VMEM, pltpu.SemaphoreType.DMA
    scratch = [
        vmem((VIEWS, FEATS, ROWS), BF16),
        vmem((gathers + 1, VIEWS, NZ, NY, OWN, K), BF16),
        vmem((reduces, VIEWS, NZ, NY, OWN, K), BF16),
        vmem((VIEWS, ROWS, K), F32),
        vmem((VIEWS, ROWS, K), BF16),
        vmem((ROWS, K), BF16),
        vmem((VIEWS, OWN, K), F32),
        vmem((VIEWS, OWN, K), F32),
        vmem((VIEWS, OWN, K), F32),
        vmem((VIEWS, OWN, K), F32),
        vmem((evals, PEERS, SROWS, K), BF16),
        vmem((evals, PEERS, SROWS, K), BF16),
        vmem((evals, ROWS, K), F32),
        vmem((evals, K, K), F32),
        vmem((evals, PEERS, GROWS, K), F32),
        vmem((evals, PEERS, GROWS, K), F32),
        vmem((evals, GROWS, K), F32),
        vmem((evals, NY, GROWS, K), F32),
        vmem((evals, GROWS, K), F32),
        vmem((evals, NZ, GROWS, K), F32),
        vmem((reduces, VIEWS, NZ, NY, MAIN, K), BF16),
        vmem((reduces, VIEWS, NZ, MAIN, K), BF16),
        vmem((reduces, VIEWS, NZ, MAIN, K), BF16),
        vmem((reduces, VIEWS, NZ, NY, REST, K), BF16),
        vmem((reduces, VIEWS, NY, REST, K), BF16),
        vmem((reduces, VIEWS, NY, REST, K), BF16),
        *[dma((1,)) for _ in range(9)],
        dma((2, VIEWS, NZ)),
        dma((2, VIEWS)),
        dma((2, VIEWS)),
        dma((2, VIEWS)),
        dma((2, VIEWS)),
        dma((VIEWS, NZ)),
        dma((VIEWS, NZ)),
        dma((VIEWS,)),
        dma((VIEWS, NZ)),
        dma((VIEWS,)),
    ]
    return pl.pallas_call(
        kernel,
        out_shape=(jax.ShapeDtypeStruct((ROWS, K), F32), jax.ShapeDtypeStruct((VIEWS, OWN, K), F32)),
        in_specs=[pl.BlockSpec(memory_space=pltpu.VMEM)] * 2,
        out_specs=(pl.BlockSpec(memory_space=pltpu.VMEM),) * 2,
        scratch_shapes=scratch,
        compiler_params=pltpu.CompilerParams(collective_id=0, has_side_effects=True, vmem_limit_bytes=56 << 20),
        name="gcca",
    )(view_data, init_coeffs)


def solution(mesh):
    in_specs = (P("view", "samp", None), P("view", None, None))
    out_specs = (P("samp", None), P("view", "samp", None))
    return jax.shard_map(body, mesh=mesh, in_specs=in_specs, out_specs=out_specs, check_vma=False)
```

time: 213 us -> 184 us (0.86)
  Pallas kernels: 209 us -> 180 us
    pallas_call x1, Pallas kernels: 209 us -> 180 us  [body(): pl.pallas_call(kernel, out_shape=(jax.ShapeDtypeStruct((ROWS, K), F32), j...]
where the time goes in v2:
time: 184 us
  Pallas kernels  180 us (98%)
  local copies, waits for them, and re-layouts  3.14 us (2%)
    pallas_call x1, Pallas kernels, body(): pl.pallas_call(kernel, out_shape=(jax.ShapeDtypeStruct((ROWS, K), F32), j...  180 us

profile of v2, /device:TPU:1, one launch (start us, length us, event | category | flops | bytes accessed | tf_op | source)
XLA Modules:
  0.0 184.2 jit_solution(2495171202434064873)
XLA Ops:
  0.6 180.4 %gcca.1 = (f32[512,128]{1,0:T(8,128)}, f32[2,64,128]{2,1,0:T(8,128)}) custom-call(bf16[2,512,2048]{2,1,0:T(8,128)(2,1)} %x_ref.1, f32[2,2048,128]{2,1,0:T(8,128)} %w_ref.1), custom_call_target="tpu_custom_call" | custom-call | tf_op jit(solution)/shard_map/gcca/pallas_call | solution.py:437
  181.0 1.7 copy.6
  182.7 1.5 copy.7

commit v3 on v2

--- a/solution.py
+++ b/solution.py
@@ -35,6 +35,11 @@
 
 def dot16(a, b):
     return jnp.dot(a, b, preferred_element_type=F32)
+
+
+def halves(a):
+    hi = a.astype(BF16)
+    return hi, (a - hi.astype(F32)).astype(BF16)
 
 
 def far_first(i):
@@ -158,8 +163,15 @@
 
         def turn(i, both):
             approx, inverse = both[:, :K], both[:, K:]
-            factor = 0.5 * (3.0 * eye - dot32(inverse, approx))
-            both = dot32(factor, both)
+            hi, lo = halves(both)
+            ah, al, ih, il = hi[:, :K], lo[:, :K], hi[:, K:], lo[:, K:]
+            none = jnp.zeros((K, K), BF16)
+            left = jnp.concatenate([ih, il], axis=1)
+            right = jnp.concatenate([jnp.concatenate([ah, al], axis=1), jnp.concatenate([ah, none], axis=1)], axis=0)
+            parts = dot16(left, right)
+            factor = 0.5 * (3.0 * eye - (parts[:, :K] + parts[:, K:]))
+            fh, fl = halves(factor)
+            both = dot16(jnp.concatenate([fh, fl], axis=1), jnp.concatenate([hi, hi], axis=0)) + dot16(fh, lo)
             if beside is not None:
                 beside(i)
             return both
@@ -330,29 +342,24 @@
             pb[member] = p[member].astype(BF16)
             rs_start(own_r, 0, member, lambda: pb[member])
         vrs_end(o)
+        rs_mid(own_r, 0, 0)
         gram_v_end(o)
+        rs_mid(own_r, 0, 1)
         vag_end(o)
         sb[...] = summed[o].astype(BF16)
-        for member in range(VIEWS):
-            rs_start(sum_r, 1, member, lambda: sb[...], both_orders=False)
+        rs_start(sum_r, 1, 0, lambda: sb[...], both_orders=False)
         gram_y_end(o)
-        for member in range(VIEWS):
-            rs_mid(own_r, 0, member)
-        for member in range(VIEWS):
-            rs_other_order(sum_r, 1, member)
+        rs_other_order(sum_r, 1, 0)
+        rs_start(sum_r, 1, 1, lambda: sb[...], both_orders=False)
+        rs_other_order(sum_r, 1, 1)
         gram_z_end(o)
-        for member in range(VIEWS):
-            rs_end(own_r, 0, member, ga)
+        rs_end(own_r, 0, 0, ga)
+        rs_end(own_r, 0, 1, ga)
+        rs_mid(sum_r, 1, 0)
         gram_end(o)
         both, scale = newton_init(o)
-
-        def beside(i):
-            for member in range(VIEWS):
-                rs_mid_step(sum_r, 1, member, i)
-
-        both = newton_turns(0, NZ, both, beside)
-        for member in range(VIEWS):
-            rs_mid_rest(sum_r, 1, member)
+        both = newton_turns(0, NZ, both, lambda i: rs_mid_step(sum_r, 1, 1, i))
+        rs_mid_rest(sum_r, 1, 1)
         both = newton_turns(NZ, NS_ITERS, both)
         white = both[:, K:] * jnp.sqrt(SAMPLES / scale)
         for member in range(VIEWS):
@@ -390,6 +397,11 @@
     both, scale = newton_init(OUTER)
     both = newton_turns(0, NS_ITERS, both)
     scores_ref[...] = dot32(summed[OUTER], both[:, K:] * jnp.sqrt(SAMPLES / scale))
+
+
+def keep(scores_ref, coeffs_ref, scores_out, coeffs_out):
+    scores_out[...] = scores_ref[...]
+    coeffs_out[...] = coeffs_ref[...]
 
 
 def body(view_data, init_coeffs):
@@ -434,7 +446,7 @@
         dma((VIEWS, NZ)),
         dma((VIEWS,)),
     ]
-    return pl.pallas_call(
+    results = pl.pallas_call(
         kernel,
         out_shape=(jax.ShapeDtypeStruct((ROWS, K), F32), jax.ShapeDtypeStruct((VIEWS, OWN, K), F32)),
         in_specs=[pl.BlockSpec(memory_space=pltpu.VMEM)] * 2,
@@ -443,6 +455,13 @@
         compiler_params=pltpu.CompilerParams(collective_id=0, has_side_effects=True, vmem_limit_bytes=56 << 20),
         name="gcca",
     )(view_data, init_coeffs)
+    return pl.pallas_call(
+        keep,
+        out_shape=(jax.ShapeDtypeStruct((ROWS, K), F32), jax.ShapeDtypeStruct((VIEWS, OWN, K), F32)),
+        in_specs=[pl.BlockSpec(memory_space=pltpu.VMEM)] * 2,
+        out_specs=(pl.BlockSpec(memory_space=pltpu.VMEM),) * 2,
+        name="keep",
+    )(*results)
 
 
 def solution(mesh):

time: 184 us -> 170 us (0.924)
  Pallas kernels: 180 us -> 169 us
  local copies, waits for them, and re-layouts: 3.14 us -> 0 us
    pallas_call x1, Pallas kernels: 180 us -> 168 us  [body(): pl.pallas_call(kernel, out_shape=(jax.ShapeDtypeStruct((ROWS, K), F32), j...]
    unnamed x2 -> x0, local copies, waits for them, and re-layouts: 3.14 us -> none
where the time goes in v3:
time: 170 us
  Pallas kernels  169 us (99%)
    pallas_call x1, Pallas kernels, body(): pl.pallas_call(kernel, out_shape=(jax.ShapeDtypeStruct((ROWS, K), F32), j...  168 us

profile of v3, /device:TPU:1, one launch (start us, length us, event | category | flops | bytes accessed | tf_op | source)
XLA Modules:
  0.0 170.0 jit_solution(4003324400711647856)
XLA Ops:
  0.6 167.7 %gcca.1 = (f32[512,128]{1,0:T(8,128)}, f32[2,64,128]{2,1,0:T(8,128)}) custom-call(bf16[2,512,2048]{2,1,0:T(8,128)(2,1)} %x_ref.1, f32[2,2048,128]{2,1,0:T(8,128)} %w_ref.1), custom_call_target="tpu_custom_call" | custom-call | tf_op jit(solution)/shard_map/gcca/pallas_call | solution.py:449
  168.3 1.7 keep.1

commit v4 on v3

--- a/solution.py
+++ b/solution.py
@@ -26,7 +26,7 @@
 PEERS = NX * NC
 SENT = (NY * NZ - 1) * OWN * K // ROWS
 GROWS = K // (NX * NC)
-SROWS = ROWS // (NX * NC)
+HALF = ROWS // NC
 
 
 def dot32(a, b):
@@ -50,15 +50,17 @@
 def kernel(
     x_ref, w_ref, scores_ref, coeffs_ref,
     xt, wb, gb, p, pb, sb, wrow, bm, ga, gs,
-    vloc, vin, summed, gram, gpart, gvin, gyout, gyin, gzout, gzin,
+    cout, cin, xin, summed, gram, gpart, gvin, gyout, gyin, gzout, gzin,
     ryin, szout, rz2in, rz1in, syout, ry2in,
-    vrs_r, vag_r, gx_r, gy_r, gz_r, gv_r, vrs_s, vag_s, gram_s,
+    core_r, core_s, vrs_r, vag_r, gx_r, gy_r, gz_r, gv_r, vrs_s, vag_s, gram_s,
     ry_r, rz2_r, rz1_r, ry2_r, rs_s,
     az_r, ayf_r, ay_r, az2_r, ag_s,
 ):
     v = lax.axis_index("view")
     s = lax.axis_index("samp")
+    x, core = v // NC, lax.rem(v, NC)
     y, z = lax.rem(s, NY), s // NY
+    sibling = {"view": v + 1 - 2 * core, "samp": s}
 
     def y_peer(m):
         return {"view": v, "samp": z * NY + lax.rem(y + m, NY)}
@@ -89,34 +91,35 @@
         pl.semaphore_signal(barrier, inc=1, device_id=v_peer(j), device_id_type=MESH)
 
     def vrs_start(t):
-        vloc[t] = (p[0] + p[1]).reshape(PEERS, SROWS, K).astype(vloc.dtype)
-        for j in range(1, PEERS):
-            to = lax.rem(v + j, PEERS)
-            copy(vloc.at[t, to], vin.at[t, j], vrs_s.at[0], vrs_r.at[0], v_peer(j)).start()
+        away = pl.ds(pl.multiple_of((1 - core) * HALF, HALF), HALF)
+        cout[t] = p[0, away] + p[1, away]
+        copy(cout.at[t], cin.at[t], core_s.at[0], core_r.at[0], sibling).start()
+
+    def vrs_mid(t):
+        here = pl.ds(pl.multiple_of(core * HALF, HALF), HALF)
+        total = p[0, here] + p[1, here]
+        arrived(cin.at[t], core_r.at[0])
+        xin[t, x] = (total + cin[t]).astype(BF16)
+        for k in (2, 1, 3):
+            copy(xin.at[t, x], xin.at[t, x], vrs_s.at[0], vrs_r.at[0], v_peer(2 * k)).start()
 
     def vrs_end(t):
-        total = vloc[t, v].astype(F32)
-        arrived(vin.at[t, pl.ds(1, PEERS - 1)], vrs_r.at[0])
-        for j in range(1, PEERS):
-            total = total + vin[t, j].astype(F32)
-        summed[t, pl.ds(v * SROWS, SROWS)] = total
+        here = pl.ds(pl.multiple_of(core * HALF, HALF), HALF)
+        arrived(xin.at[t, pl.ds(0, NX - 1)], vrs_r.at[0])
+        total = xin[t, 0].astype(F32)
+        for k in range(1, NX):
+            total = total + xin[t, k].astype(F32)
+        summed[t, here] = total
         gpart[t] = dot32(total.T, total).reshape(PEERS, GROWS, K)
-        for j in range(1, PEERS):
-            to = lax.rem(v + j, PEERS)
-            copy(gpart.at[t, to], gvin.at[t, j], gram_s.at[0], gx_r.at[0], v_peer(j)).start()
-        block = summed.at[t, pl.ds(v * SROWS, SROWS)]
-        for j in range(1, PEERS):
-            copy(block, block, vag_s.at[0], vag_r.at[0], v_peer(j)).start()
+        copy(gpart.at[t, v + 1 - 2 * core], gvin.at[t], gram_s.at[0], gx_r.at[0], sibling).start()
+        copy(summed.at[t, here], summed.at[t, here], vag_s.at[0], vag_r.at[0], sibling).start()
 
     def vag_end(t):
-        arrived(summed.at[t, pl.ds(0, ROWS - SROWS)], vag_r.at[0])
+        arrived(summed.at[t, pl.ds(0, HALF)], vag_r.at[0])
 
     def gram_v_end(t):
-        total = gpart[t, v]
-        arrived(gvin.at[t, pl.ds(1, PEERS - 1)], gx_r.at[0])
-        for j in range(1, PEERS):
-            total = total + gvin[t, j]
-        gyout[t] = total
+        arrived(gvin.at[t], gx_r.at[0])
+        gyout[t] = gpart[t, v] + gvin[t]
         for m in range(1, NY):
             copy(gyout.at[t], gyin.at[t, m], gram_s.at[0], gy_r.at[0], y_peer(m)).start()
 
@@ -141,9 +144,10 @@
 
     def gram_end(t):
         arrived(gram.at[t, pl.ds(0, K - GROWS)], gv_r.at[0])
-        sent(vin.at[t, pl.ds(1, PEERS - 1)], vrs_s.at[0])
-        sent(summed.at[t, pl.ds(0, ROWS - SROWS)], vag_s.at[0])
-        sent(summed.at[t, pl.ds(0, (3 * 7 + 3) * GROWS)], gram_s.at[0])
+        sent(cout.at[t], core_s.at[0])
+        sent(xin.at[t, pl.ds(0, NX - 1)], vrs_s.at[0])
+        sent(summed.at[t, pl.ds(0, HALF)], vag_s.at[0])
+        sent(summed.at[t, pl.ds(0, (NY + NZ + PEERS - 2) * GROWS)], gram_s.at[0])
 
     def eye_mat():
         row = lax.broadcasted_iota(jnp.int32, (K, K), 0)
@@ -275,15 +279,15 @@
         block = wb.at[a, member, z, y, pl.ds(MAIN, REST)]
         for m in range(1, NY):
             copy(block, block, ag_s.at[member], ay_r.at[member], y_peer(m)).start()
+        ayf_start(a, member, 0)
         block = wb.at[a, member, z, y, pl.ds(0, MAIN)]
         for j in (1, 7, 2, 6, 3, 5, 4):
             copy(block, block, ag_s.at[member], az_r.at[member, j], z_peer(j)).start()
-        ayf_start(a, member, 0)
 
     def gather_forward(a, member):
         arrived(wb.at[a, member, z, pl.ds(0, NY - 1), pl.ds(0, REST)], ay_r.at[member])
         block = wb.at[a, member, z, :, pl.ds(MAIN, REST)]
-        for j in (4, 5, 3, 6, 2, 7, 1):
+        for j in (1, 7, 2, 6, 3, 5, 4):
             copy(block, block, ag_s.at[member], az2_r.at[member, j], z_peer(j)).start()
 
         def forward(i, _):
@@ -338,17 +342,19 @@
         own_r, sum_r, next_r = 3 * o, 3 * o + 1, 3 * o + 2
         one, two = 2 * o + 1, 2 * o + 2
         vrs_start(o)
-        for member in range(VIEWS):
-            pb[member] = p[member].astype(BF16)
-            rs_start(own_r, 0, member, lambda: pb[member])
+        pb[0] = p[0].astype(BF16)
+        rs_start(own_r, 0, 0, lambda: pb[0])
+        vrs_mid(o)
+        pb[1] = p[1].astype(BF16)
+        rs_start(own_r, 0, 1, lambda: pb[1])
         vrs_end(o)
+        gram_v_end(o)
         rs_mid(own_r, 0, 0)
-        gram_v_end(o)
-        rs_mid(own_r, 0, 1)
         vag_end(o)
         sb[...] = summed[o].astype(BF16)
         rs_start(sum_r, 1, 0, lambda: sb[...], both_orders=False)
         gram_y_end(o)
+        rs_mid(own_r, 0, 1)
         rs_other_order(sum_r, 1, 0)
         rs_start(sum_r, 1, 1, lambda: sb[...], both_orders=False)
         rs_other_order(sum_r, 1, 1)
@@ -388,6 +394,7 @@
     lax.fori_loop(0, OUTER, outer, 0)
     vrs_start(OUTER)
     coeffs_ref[...] = wrow[...]
+    vrs_mid(OUTER)
     vrs_end(OUTER)
     gram_v_end(OUTER)
     gram_y_end(OUTER)
@@ -418,12 +425,13 @@
         vmem((VIEWS, OWN, K), F32),
         vmem((VIEWS, OWN, K), F32),
         vmem((VIEWS, OWN, K), F32),
-        vmem((evals, PEERS, SROWS, K), BF16),
-        vmem((evals, PEERS, SROWS, K), BF16),
+        vmem((evals, HALF, K), F32),
+        vmem((evals, HALF, K), F32),
+        vmem((evals, NX, HALF, K), BF16),
         vmem((evals, ROWS, K), F32),
         vmem((evals, K, K), F32),
         vmem((evals, PEERS, GROWS, K), F32),
-        vmem((evals, PEERS, GROWS, K), F32),
+        vmem((evals, GROWS, K), F32),
         vmem((evals, GROWS, K), F32),
         vmem((evals, NY, GROWS, K), F32),
         vmem((evals, GROWS, K), F32),
@@ -434,7 +442,7 @@
         vmem((reduces, VIEWS, NZ, NY, REST, K), BF16),
         vmem((reduces, VIEWS, NY, REST, K), BF16),
         vmem((reduces, VIEWS, NY, REST, K), BF16),
-        *[dma((1,)) for _ in range(9)],
+        *[dma((1,)) for _ in range(11)],
         dma((2, VIEWS, NZ)),
         dma((2, VIEWS)),
         dma((2, VIEWS)),

time: 170 us -> 166 us (0.976)
  Pallas kernels: 169 us -> 165 us
    pallas_call x1, Pallas kernels: 168 us -> 163 us  [body(): pl.pallas_call(kernel, out_shape=(jax.ShapeDtypeStruct((ROWS, K), F32), j...]
where the time goes in v4:
time: 166 us
  Pallas kernels  165 us (99%)
    pallas_call x1, Pallas kernels, body(): pl.pallas_call(kernel, out_shape=(jax.ShapeDtypeStruct((ROWS, K), F32), j...  163 us

profile of v4, /device:TPU:1, one launch (start us, length us, event | category | flops | bytes accessed | tf_op | source)
XLA Modules:
  0.0 165.6 jit_solution(2728813830583604850)
XLA Ops:
  0.6 163.3 %gcca.1 = (f32[512,128]{1,0:T(8,128)}, f32[2,64,128]{2,1,0:T(8,128)}) custom-call(bf16[2,512,2048]{2,1,0:T(8,128)(2,1)} %x_ref.1, f32[2,2048,128]{2,1,0:T(8,128)} %w_ref.1), custom_call_target="tpu_custom_call" | custom-call | tf_op jit(solution)/shard_map/gcca/pallas_call | solution.py:457
  163.9 1.7 %keep.1 = (f32[512,128]{1,0:T(8,128)}, f32[2,64,128]{2,1,0:T(8,128)}) custom-call(f32[512,128]{1,0:T(8,128)} %get-tuple-element.4.scores_ref, f32[2,64,128]{2,1,0:T(8,128)} %get-tuple-element.5.coeffs_ref), custom_call_target="tpu_custom_call" | custom-call | tf_op jit(solution)/shard_map/keep/pallas_call | solution.py:466

commit v5 on v4

--- a/solution.py
+++ b/solution.py
@@ -48,13 +48,13 @@
 
 
 def kernel(
-    x_ref, w_ref, scores_ref, coeffs_ref,
-    xt, wb, gb, p, pb, sb, wrow, bm, ga, gs,
+    x_hbm, w_ref, scores_ref, coeffs_ref,
+    x_ref, xt, wb, gb, p, pb, sb, wrow, bm, ga, gs,
     cout, cin, xin, summed, gram, gpart, gvin, gyout, gyin, gzout, gzin,
     ryin, szout, rz2in, rz1in, syout, ry2in,
     core_r, core_s, vrs_r, vag_r, gx_r, gy_r, gz_r, gv_r, vrs_s, vag_s, gram_s,
     ry_r, rz2_r, rz1_r, ry2_r, rs_s,
-    az_r, ayf_r, ay_r, az2_r, ag_s,
+    az_r, ayf_r, ay_r, az2_r, ag_s, load_s,
 ):
     v = lax.axis_index("view")
     s = lax.axis_index("samp")
@@ -81,6 +81,13 @@
 
     def sent(ref, send):
         copy(ref, ref, send, ay_r.at[0], y_peer(1)).wait_send()
+
+    def load(i):
+        cols = pl.ds(pl.multiple_of(i * BLOCK, BLOCK), BLOCK)
+        return pltpu.make_async_copy(x_hbm.at[:, :, cols], x_ref.at[:, :, cols], load_s.at[i])
+
+    for i in range(NZ):
+        load(i).start()
 
     barrier = pltpu.get_barrier_semaphore()
     for m in range(1, NY):
@@ -329,13 +336,14 @@
     p[...] = jnp.zeros_like(p)
 
     def first(i, _):
+        load(i).wait()
         cols = pl.ds(pl.multiple_of(i * BLOCK, BLOCK), BLOCK)
         for member in range(VIEWS):
             product_of(0, member, i)
             xt[member, cols, :] = x_ref[member, :, cols].T
         return 0
 
-    lax.fori_loop(0, NZ, first, 0)
+    lax.fori_loop(0, NZ, first, 0, unroll=2)
     pl.semaphore_wait(barrier, (NY - 1) + (NZ - 1) + (PEERS - 1))
 
     def outer(o, _):
@@ -350,11 +358,11 @@
         vrs_end(o)
         gram_v_end(o)
         rs_mid(own_r, 0, 0)
+        rs_mid(own_r, 0, 1)
         vag_end(o)
         sb[...] = summed[o].astype(BF16)
         rs_start(sum_r, 1, 0, lambda: sb[...], both_orders=False)
         gram_y_end(o)
-        rs_mid(own_r, 0, 1)
         rs_other_order(sum_r, 1, 0)
         rs_start(sum_r, 1, 1, lambda: sb[...], both_orders=False)
         rs_other_order(sum_r, 1, 1)
@@ -415,6 +423,7 @@
     evals, reduces, gathers = OUTER + 1, 3 * OUTER, 2 * OUTER
     vmem, dma = pltpu.VMEM, pltpu.SemaphoreType.DMA
     scratch = [
+        vmem((VIEWS, ROWS, FEATS), BF16),
         vmem((VIEWS, FEATS, ROWS), BF16),
         vmem((gathers + 1, VIEWS, NZ, NY, OWN, K), BF16),
         vmem((reduces, VIEWS, NZ, NY, OWN, K), BF16),
@@ -453,11 +462,12 @@
         dma((VIEWS,)),
         dma((VIEWS, NZ)),
         dma((VIEWS,)),
+        dma((NZ,)),
     ]
     results = pl.pallas_call(
         kernel,
         out_shape=(jax.ShapeDtypeStruct((ROWS, K), F32), jax.ShapeDtypeStruct((VIEWS, OWN, K), F32)),
-        in_specs=[pl.BlockSpec(memory_space=pltpu.VMEM)] * 2,
+        in_specs=[pl.BlockSpec(memory_space=pl.ANY), pl.BlockSpec(memory_space=pltpu.VMEM)],
         out_specs=(pl.BlockSpec(memory_space=pltpu.VMEM),) * 2,
         scratch_shapes=scratch,
         compiler_params=pltpu.CompilerParams(collective_id=0, has_side_effects=True, vmem_limit_bytes=56 << 20),

time: 166 us -> 165 us (level)
  no operation moved by 1% of the time
where the time goes in v5:
time: 165 us
  Pallas kernels  164 us (99%)
    pallas_call x1, Pallas kernels, body(): pl.pallas_call(kernel, out_shape=(jax.ShapeDtypeStruct((ROWS, K), F32), j...  163 us

profile of v5, /device:TPU:1, one launch (start us, length us, event | category | flops | bytes accessed | tf_op | source)
XLA Modules:
  0.0 164.9 jit_solution(8336301934963378309)
XLA Ops:
  0.6 162.6 %gcca.1 = (f32[512,128]{1,0:T(8,128)}, f32[2,64,128]{2,1,0:T(8,128)}) custom-call(bf16[2,512,2048]{2,1,0:T(8,128)(2,1)} %x_hbm.1, f32[2,2048,128]{2,1,0:T(8,128)} %w_ref.1), custom_call_target="tpu_custom_call" | custom-call | tf_op jit(solution)/shard_map/gcca/pallas_call | solution.py:467
  163.3 1.7 %keep.1 = (f32[512,128]{1,0:T(8,128)}, f32[2,64,128]{2,1,0:T(8,128)}) custom-call(f32[512,128]{1,0:T(8,128)} %get-tuple-element.4.scores_ref, f32[2,64,128]{2,1,0:T(8,128)} %get-tuple-element.5.coeffs_ref), custom_call_target="tpu_custom_call" | custom-call | tf_op jit(solution)/shard_map/keep/pallas_call | solution.py:476

commit v6 on v5

--- a/solution.py
+++ b/solution.py
@@ -191,7 +191,7 @@
 
     def ry_start(r, q, member, j):
         to_z = lax.rem(z + j, NZ)
-        for m in range(1, NY):
+        for m in (2, 1, 3):
             to_y = lax.rem(y + m, NY)
             copy(
                 gb.at[r, member, to_z, to_y, pl.ds(0, MAIN)], ryin.at[r, member, j, m],
@@ -278,7 +278,7 @@
     def ayf_start(a, member, j):
         from_z = lax.rem(z - j + NZ, NZ)
         block = wb.at[a, member, from_z, y, pl.ds(0, MAIN)]
-        for m in range(1, NY):
+        for m in (2, 1, 3):
             copy(block, block, ag_s.at[member], ayf_r.at[member, j], y_peer(m)).start()
 
     def gather_start(a, member):

time: 165 us -> 165 us (level)
  no operation moved by 1% of the time
where the time goes in v6:
time: 165 us
  Pallas kernels  164 us (99%)
    pallas_call x1, Pallas kernels, body(): pl.pallas_call(kernel, out_shape=(jax.ShapeDtypeStruct((ROWS, K), F32), j...  162 us

profile of v6, /device:TPU:1, one launch (start us, length us, event | category | flops | bytes accessed | tf_op | source)
XLA Modules:
  0.0 164.6 jit_solution(3221587984068680440)
XLA Ops:
  0.6 162.3 %gcca.1 = (f32[512,128]{1,0:T(8,128)}, f32[2,64,128]{2,1,0:T(8,128)}) custom-call(bf16[2,512,2048]{2,1,0:T(8,128)(2,1)} %x_hbm.1, f32[2,2048,128]{2,1,0:T(8,128)} %w_ref.1), custom_call_target="tpu_custom_call" | custom-call | tf_op jit(solution)/shard_map/gcca/pallas_call | solution.py:467
  162.9 1.7 %keep.1 = (f32[512,128]{1,0:T(8,128)}, f32[2,64,128]{2,1,0:T(8,128)}) custom-call(f32[512,128]{1,0:T(8,128)} %get-tuple-element.4.scores_ref, f32[2,64,128]{2,1,0:T(8,128)} %get-tuple-element.5.coeffs_ref), custom_call_target="tpu_custom_call" | custom-call | tf_op jit(solution)/shard_map/keep/pallas_call | solution.py:476
